TPU v7x, 32 devices: a whole 2x2x4 slice. The times are simulated.
32 devices in a mesh: groups: 2 (over y), chan: 16 (over z, x, core).
Axes of the slice: x: 2, y: 2, z: 4, core: 2. Of those that a mesh axis runs over, the one named last changes fastest.
Arguments:
- record: bfloat16 [2048, 12288], P(('groups', 'chan')), parts along dimension 0, may hold values from -2000 to 2000
- starts: int32 [4], P('groups'), parts along dimension 0, may hold values from 0 to 8192, as said below
- send_rows: int32 [32, 16, 2], P(('groups', 'chan')), parts along dimension 0, may hold values from 0 to 63, as said below
- send_count: int32 [32, 16], P(('groups', 'chan')), parts along dimension 0, may hold values from 0 to 2, as said below
- pair_slots: int32 [2, 16384], P(None, ('groups', 'chan')), parts along dimension 1, may hold values from -1 to 31, as said below
- pair_count: int32 [32], P(('groups', 'chan')), parts along dimension 0, may hold values from 1 to 512, as said below
Outputs:
- correlations: float32 [16384, 512], P(('groups', 'chan')), parts along dimension 0
There are 2 independent parts, one for each index of `groups`. A program takes and returns all parts, laid end to end along the dimension named above; each array names one. Nothing has to cross between parts.
Inputs may be any that keep to these rules, and one draw needn't show every extreme that they name: Window starts never fall. `send_rows`: local channel numbers; the slots of one device to one owner name distinct channels. `send_count`: some owner receives 2 rows from every device; every device sends at least one row to itself as owner. `pair_count`: each owner has at least as many live pairs as it receives live rows; some owner has 512. `pair_slots`: a live pair names two live slots of its owner, distinct where the owner has two or more live slots; every live slot is named by some pair; entries of pairs at or beyond pair_count are -1.
All inputs are finite; a program needn't handle non-finite values.
Results may differ from a plain program's by a relative error of at most 0.0059.
Values may be sent and summed in bfloat16 or wider, within the bound.
A program may use at most 192 MiB of HBM per device.

v0:
```python
import math

import jax
import jax.numpy as jnp
from jax import lax
from jax.sharding import PartitionSpec as P

F = 2048
WLEN = 4096
BAND = 64
LAGS = 512


def taper_window():
    samples = jnp.arange(WLEN, dtype=jnp.float32)
    return 0.5 - 0.5 * jnp.cos(2.0 * math.pi / WLEN * samples)


def dft_block(first_bin, width):
    sample_idx = jnp.arange(WLEN, dtype=jnp.int32)[:, None]
    bin_idx = first_bin + jnp.arange(width, dtype=jnp.int32)[None, :]
    phases = (sample_idx * bin_idx % WLEN).astype(jnp.float32) * (2.0 * math.pi / WLEN)
    return (jnp.cos(phases).astype(jnp.bfloat16), (-jnp.sin(phases)).astype(jnp.bfloat16))


def lag_table():
    bin_idx = jnp.arange(F, dtype=jnp.int32)[:, None]
    shifts = (jnp.arange(LAGS, dtype=jnp.int32) - LAGS // 2) % WLEN
    phases = (bin_idx * shifts[None, :] % WLEN).astype(jnp.float32) * (2.0 * math.pi / WLEN)
    factor = 1.0 / math.sqrt(F)
    return jnp.concatenate([jnp.cos(phases) * factor, -jnp.sin(phases) * factor], axis=0).astype(
        jnp.bfloat16
    )


def whiten(real_part, imag_part):
    leading = real_part.shape[:-1]
    bands = F // BAND
    powers = real_part * real_part + imag_part * imag_part
    band_power = powers.reshape(leading + (bands, BAND)).sum(-1) / (2.0 * BAND)
    scales = (1.0 / jnp.sqrt(band_power + 1e-06))[..., None]
    real_white = (real_part.reshape(leading + (bands, BAND)) * scales).reshape(leading + (F,))
    imag_white = (imag_part.reshape(leading + (bands, BAND)) * scales).reshape(leading + (F,))
    return jnp.concatenate([real_white, imag_white], axis=-1).astype(jnp.bfloat16)


def windows_of(record, starts):
    taper_win = taper_window()
    pieces = jax.vmap(lambda offset: lax.dynamic_slice_in_dim(record, offset, WLEN, 1))(starts)
    return (pieces.astype(jnp.float32) * taper_win).astype(jnp.bfloat16)


def accumulate(running, arrived_rows, first_slot, second_slot):
    real_acc, imag_acc = running
    rows_a = jnp.take(arrived_rows, first_slot, axis=0).astype(jnp.float32)
    rows_b = jnp.take(arrived_rows, second_slot, axis=0).astype(jnp.float32)
    half_width = rows_a.shape[1] // 2
    real_a, imag_a = (rows_a[:, :half_width], rows_a[:, half_width:])
    real_b, imag_b = (rows_b[:, :half_width], rows_b[:, half_width:])
    return (
        real_acc + (real_a * real_b + imag_a * imag_b),
        imag_acc + (imag_a * real_b - real_a * imag_b),
    )


def body(record, starts, send_rows, send_count, pair_slots, pair_count):
    local_chan = record.shape[0]
    windows = starts.shape[0]
    devices = lax.axis_size("chan")
    segments = windows_of(record, starts)
    flat_rows = segments.reshape(windows * local_chan, WLEN)
    block_width = min(256, F)
    real_parts = []
    imag_parts = []
    for first_bin in range(0, F, block_width):
        cos_tab, sin_tab = dft_block(first_bin, block_width)
        real_block = jnp.dot(flat_rows, cos_tab, preferred_element_type=jnp.float32).reshape(
            windows, local_chan, block_width
        )
        imag_block = jnp.dot(flat_rows, sin_tab, preferred_element_type=jnp.float32).reshape(
            windows, local_chan, block_width
        )
        real_parts.append(real_block)
        imag_parts.append(imag_block)
    real_part = jnp.concatenate(real_parts, axis=2)
    imag_part = jnp.concatenate(imag_parts, axis=2)
    mode_real_all, mode_imag_all = lax.psum(
        (jnp.sum(real_part, axis=1), jnp.sum(imag_part, axis=1)), "chan"
    )
    total_chan = local_chan * devices
    real_part = real_part - mode_real_all[:, None, :] / total_chan
    imag_part = imag_part - mode_imag_all[:, None, :] / total_chan
    whitened = whiten(real_part, imag_part)
    dest_rows = send_rows[0]
    dest_count = send_count[0]
    cap_slots = dest_rows.shape[1]
    flat_dest = dest_rows.reshape(-1)
    slot_live = jnp.arange(cap_slots, dtype=jnp.int32)[None, :] < dest_count[:, None]
    first_slot = jnp.maximum(pair_slots[0], 0)
    second_slot = jnp.maximum(pair_slots[1], 0)
    pair_cap = pair_slots.shape[1]
    zero_acc = jnp.zeros((pair_cap, F), jnp.float32)
    width_two = 2 * F
    outgoing = jnp.take(whitened, flat_dest, axis=1).reshape(windows, devices, cap_slots, width_two)
    outgoing = jnp.where(slot_live[None, :, :, None], outgoing, jnp.zeros_like(outgoing))
    incoming = lax.all_to_all(outgoing, "chan", split_axis=1, concat_axis=1, tiled=True).reshape(
        windows, devices * cap_slots, width_two
    )

    def window_step(window_idx, running):
        slab_rows = lax.dynamic_index_in_dim(incoming, window_idx, 0, keepdims=False)
        return accumulate(running, slab_rows, first_slot, second_slot)

    cross_real, cross_imag = lax.fori_loop(0, windows, window_step, (zero_acc, zero_acc))
    cross_spec = jnp.concatenate([cross_real / windows, cross_imag / windows], axis=1).astype(
        jnp.bfloat16
    )
    lag_tab = lag_table()
    live_pairs = pair_count[0]
    lagged = jnp.dot(cross_spec, lag_tab, preferred_element_type=jnp.float32)
    is_alive = jnp.arange(pair_cap, dtype=jnp.int32) < live_pairs
    lagged = jnp.where(is_alive[:, None], lagged, jnp.zeros_like(lagged))
    return lagged


def solution(mesh):
    in_specs = (
        P(("groups", "chan"), None),
        P("groups"),
        P(("groups", "chan"), None, None),
        P(("groups", "chan"), None),
        P(None, ("groups", "chan")),
        P(("groups", "chan")),
    )
    out_specs = P(("groups", "chan"), None)
    return jax.shard_map(body, mesh=mesh, in_specs=in_specs, out_specs=out_specs, check_vma=False)
```

profile of v0, /device:TPU:0, one launch (start us, length us, event | category | flops | bytes accessed | tf_op | source)
XLA Modules:
  0.0 481.7 jit_solution(14975516556051533183)
XLA Ops:
  5.9 16.4 %constant_dynamic-update-slice_fusion.7 = (f32[2,64,2048]{2,1,0:T(8,128)S(1)}, f32[2,64,256]{2,1,0:T(8,128)}) fusion(bf16[2,64,4096]{2,1,0:T(8,128)(2,1)S(1)} %get-tuple-element.125, f32[4096]{0:T(1024)S(1)} %multiply_subtract_fusion), kind=kOutput, calls=%fused_computation.175 | convolution fusion | flops 285736960 | bytes 1327104 | tf_op jit(solution)/shard_map/dot_general | solution.py:77
  22.3 16.7 %constant_dynamic-update-slice_fusion.15 = (f32[2,64,2048]{2,1,0:T(8,128)S(1)}, f32[2,64,256]{2,1,0:T(8,128)}) fusion(bf16[2,64,4096]{2,1,0:T(8,128)(2,1)S(1)} %get-tuple-element.125, f32[4096]{0:T(1024)S(1)} %multiply_subtract_fusion), kind=kOutput, calls=%fused_computation.183 | convolution fusion | flops 286785536 | bytes 1327104 | tf_op jit(solution)/shard_map/dot_general | solution.py:80
  39.0 16.7 %constant_dynamic-update-slice_fusion.6 = (f32[2,64,2048]{2,1,0:T(8,128)S(1)}, f32[2,64,256]{2,1,0:T(8,128)}) fusion(f32[2,64,2048]{2,1,0:T(8,128)S(1)} %get-tuple-element.213, s32[256]{0:T(256)S(1)} %iota_add_fusion.6, bf16[2,64,4096]{2,1,0:T(8,128)(2,1)S(1)} %get-tuple-element.125, f32[4096]{0:T(1024)S(1)} %multiply_subtract_fusion), kind=kOutput, calls=%fused_computation.174 | convolution fusion | flops 285736960 | bytes 1328128 | tf_op jit(solution)/shard_map/dot_general | solution.py:77
  55.8 16.6 %constant_dynamic-update-slice_fusion.14 = (f32[2,64,2048]{2,1,0:T(8,128)S(1)}, f32[2,64,256]{2,1,0:T(8,128)}) fusion(f32[2,64,2048]{2,1,0:T(8,128)S(1)} %get-tuple-element.197, s32[256]{0:T(256)S(1)} %iota_add_fusion.6, bf16[2,64,4096]{2,1,0:T(8,128)(2,1)S(1)} %get-tuple-element.125, f32[4096]{0:T(1024)S(1)} %multiply_subtract_fusion), kind=kOutput, calls=%fused_computation.182 | convolution fusion | flops 286785536 | bytes 1328128 | tf_op jit(solution)/shard_map/dot_general | solution.py:80
  72.4 16.5 %constant_dynamic-update-slice_fusion.5 = (f32[2,64,2048]{2,1,0:T(8,128)S(1)}, f32[2,64,256]{2,1,0:T(8,128)}) fusion(f32[2,64,2048]{2,1,0:T(8,128)S(1)} %get-tuple-element.215, s32[256]{0:T(256)S(1)} %iota_add_fusion.5, bf16[2,64,4096]{2,1,0:T(8,128)(2,1)S(1)} %get-tuple-element.125, f32[4096]{0:T(1024)S(1)} %multiply_subtract_fusion), kind=kOutput, calls=%fused_computation.173 | convolution fusion | flops 285736960 | bytes 1328128 | tf_op jit(solution)/shard_map/dot_general | solution.py:77
  89.0 16.8 %constant_dynamic-update-slice_fusion.13 = (f32[2,64,2048]{2,1,0:T(8,128)S(1)}, f32[2,64,256]{2,1,0:T(8,128)}) fusion(f32[2,64,2048]{2,1,0:T(8,128)S(1)} %get-tuple-element.199, s32[256]{0:T(256)S(1)} %iota_add_fusion.5, bf16[2,64,4096]{2,1,0:T(8,128)(2,1)S(1)} %get-tuple-element.125, f32[4096]{0:T(1024)S(1)} %multiply_subtract_fusion), kind=kOutput, calls=%fused_computation.181 | convolution fusion | flops 286785536 | bytes 1328128 | tf_op jit(solution)/shard_map/dot_general | solution.py:80
  105.7 16.6 %constant_dynamic-update-slice_fusion.4 = (f32[2,64,2048]{2,1,0:T(8,128)S(1)}, f32[2,64,256]{2,1,0:T(8,128)}) fusion(f32[2,64,2048]{2,1,0:T(8,128)S(1)} %get-tuple-element.217, s32[256]{0:T(256)S(1)} %iota_add_fusion.4, bf16[2,64,4096]{2,1,0:T(8,128)(2,1)S(1)} %get-tuple-element.125, f32[4096]{0:T(1024)S(1)} %multiply_subtract_fusion), kind=kOutput, calls=%fused_computation.172 | convolution fusion | flops 285736960 | bytes 1328128 | tf_op jit(solution)/shard_map/dot_general | solution.py:77
  122.3 16.6 %constant_dynamic-update-slice_fusion.12 = (f32[2,64,2048]{2,1,0:T(8,128)S(1)}, f32[2,64,256]{2,1,0:T(8,128)}) fusion(f32[2,64,2048]{2,1,0:T(8,128)S(1)} %get-tuple-element.201, s32[256]{0:T(256)S(1)} %iota_add_fusion.4, bf16[2,64,4096]{2,1,0:T(8,128)(2,1)S(1)} %get-tuple-element.125, f32[4096]{0:T(1024)S(1)} %multiply_subtract_fusion), kind=kOutput, calls=%fused_computation.180 | convolution fusion | flops 286785536 | bytes 1328128 | tf_op jit(solution)/shard_map/dot_general | solution.py:80
  138.9 16.1 %constant_dynamic-update-slice_fusion.3 = (f32[2,64,2048]{2,1,0:T(8,128)S(1)}, f32[2,64,256]{2,1,0:T(8,128)S(1)}) fusion(f32[2,64,2048]{2,1,0:T(8,128)S(1)} %get-tuple-element.219, s32[256]{0:T(256)S(1)} %iota_add_fusion.3, bf16[2,64,4096]{2,1,0:T(8,128)(2,1)S(1)} %get-tuple-element.125, f32[4096]{0:T(1024)S(1)} %multiply_subtract_fusion), kind=kOutput, calls=%fused_computation.171 | convolution fusion | flops 285736960 | bytes 1328128 | tf_op jit(solution)/shard_map/dot_general | solution.py:77
  155.0 16.6 %constant_dynamic-update-slice_fusion.11 = (f32[2,64,2048]{2,1,0:T(8,128)S(1)}, f32[2,64,256]{2,1,0:T(8,128)}) fusion(f32[2,64,2048]{2,1,0:T(8,128)S(1)} %get-tuple-element.203, s32[256]{0:T(256)S(1)} %iota_add_fusion.3, bf16[2,64,4096]{2,1,0:T(8,128)(2,1)S(1)} %get-tuple-element.125, f32[4096]{0:T(1024)S(1)} %multiply_subtract_fusion), kind=kOutput, calls=%fused_computation.179 | convolution fusion | flops 286785536 | bytes 1328128 | tf_op jit(solution)/shard_map/dot_general | solution.py:80
  171.6 15.7 %constant_dynamic-update-slice_fusion.2 = (f32[2,64,2048]{2,1,0:T(8,128)S(1)}, f32[2,64,256]{2,1,0:T(8,128)S(1)}) fusion(f32[2,64,2048]{2,1,0:T(8,128)S(1)} %get-tuple-element.221, s32[256]{0:T(256)S(1)} %iota_add_fusion.2, bf16[2,64,4096]{2,1,0:T(8,128)(2,1)S(1)} %get-tuple-element.125, f32[4096]{0:T(1024)S(1)} %multiply_subtract_fusion), kind=kOutput, calls=%fused_computation.170 | convolution fusion | flops 285736960 | bytes 1328128 | tf_op jit(solution)/shard_map/dot_general | solution.py:77
  187.3 17.4 %constant_dynamic-update-slice_fusion.10 = (f32[2,64,2048]{2,1,0:T(8,128)S(1)}, f32[2,64,256]{2,1,0:T(8,128)}) fusion(f32[2,64,2048]{2,1,0:T(8,128)S(1)} %get-tuple-element.205, s32[256]{0:T(256)S(1)} %iota_add_fusion.2, bf16[2,64,4096]{2,1,0:T(8,128)(2,1)S(1)} %get-tuple-element.125, f32[4096]{0:T(1024)S(1)} %multiply_subtract_fusion), kind=kOutput, calls=%fused_computation.178 | convolution fusion | flops 286785536 | bytes 1328128 | tf_op jit(solution)/shard_map/dot_general | solution.py:80
  204.7 18.9 %constant_dynamic-update-slice_fusion.1 = (f32[2,64,2048]{2,1,0:T(8,128)S(1)}, f32[2,64,256]{2,1,0:T(8,128)S(1)}) fusion(f32[2,64,2048]{2,1,0:T(8,128)S(1)} %get-tuple-element.223, s32[256]{0:T(256)S(1)} %iota_add_fusion.1, bf16[2,64,4096]{2,1,0:T(8,128)(2,1)} %copy-done.7, f32[4096]{0:T(1024)S(1)} %multiply_subtract_fusion), kind=kOutput, calls=%fused_computation.169 | convolution fusion | flops 285736960 | bytes 1328128 | tf_op jit(solution)/shard_map/dot_general | solution.py:77
  223.6 16.8 %constant_dynamic-update-slice_fusion.9 = (f32[2,64,2048]{2,1,0:T(8,128)S(1)}, f32[2,64,256]{2,1,0:T(8,128)}) fusion(f32[2,64,2048]{2,1,0:T(8,128)S(1)} %get-tuple-element.207, s32[256]{0:T(256)S(1)} %iota_add_fusion.1, bf16[2,64,4096]{2,1,0:T(8,128)(2,1)S(1)} %copy-done.8, f32[4096]{0:T(1024)S(1)} %multiply_subtract_fusion), kind=kOutput, calls=%fused_computation.177 | convolution fusion | flops 286785536 | bytes 1328128 | tf_op jit(solution)/shard_map/dot_general | solution.py:80
  240.4 15.7 %constant_dynamic-update-slice_fusion = (f32[2,64,2048]{2,1,0:T(8,128)S(1)}, f32[2,64,256]{2,1,0:T(8,128)S(1)}) fusion(f32[2,64,2048]{2,1,0:T(8,128)S(1)} %get-tuple-element.225, s32[256]{0:T(256)S(1)} %iota_add_fusion, bf16[2,64,4096]{2,1,0:T(8,128)(2,1)S(1)} %copy-done.8, f32[4096]{0:T(1024)S(1)} %multiply_subtract_fusion), kind=kOutput, calls=%fused_computation.168 | convolution fusion | flops 285736960 | bytes 1328128 | tf_op jit(solution)/shard_map/dot_general | solution.py:77
  256.1 17.0 %constant_dynamic-update-slice_fusion.8 = (f32[2,64,2048]{2,1,0:T(8,128)S(1)}, f32[2,64,256]{2,1,0:T(8,128)}) fusion(f32[2,64,2048]{2,1,0:T(8,128)S(1)} %get-tuple-element.209, s32[256]{0:T(256)S(1)} %iota_add_fusion, bf16[2,64,4096]{2,1,0:T(8,128)(2,1)S(1)} %copy-done.8, f32[4096]{0:T(1024)S(1)} %multiply_subtract_fusion), kind=kOutput, calls=%fused_computation.176 | convolution fusion | flops 286785536 | bytes 1328128 | tf_op jit(solution)/shard_map/dot_general | solution.py:80
  273.3 62.9 %all-reduce.1 = (f32[2,2048]{1,0:T(2,128)S(1)}, f32[2,2048]{1,0:T(2,128)S(1)}) all-reduce(f32[2,2048]{1,0:T(2,128)S(1)} %reduce_sum.28, f32[2,2048]{1,0:T(2,128)S(1)} %reduce_sum.27), channel_id=1, replica_groups=mesh['groups'=2,'chan'=16] {'chan'}, use_global_device_ids=true, to_apply=%region_3.4 | all-reduce | flops 8192 | bytes 65536 | tf_op jit(solution)/shard_map/psum | solution.py:87
  360.1 7.6 %concatenate.85 = f32[2,64,32,64]{3,2,1,0:T(8,128)} concatenate(f32[2,64,4,64]{3,2,1,0:T(4,128)} %concatenate.77, f32[2,64,4,64]{3,2,1,0:T(4,128)} %concatenate.78, f32[2,64,4,64]{3,2,1,0:T(4,128)} %concatenate.79, f32[2,64,4,64]{3,2,1,0:T(4,128)} %concatenate.80, f32[2,64,4,64]{3,2,1,0:T(4,128)} %concatenate.81, f32[2,64,4,64]{3,2,1,0:T(4,128)} %concatenate.82, ...), dimensions={2} | concatenate | bytes 2097152 | tf_op jit(solution)/shard_map/concatenate | solution.py:86
  388.8 18.4 %multiply_convert_fusion.1 = (bf16[2048,512]{1,0:T(8,128)(2,1)}, bf16[2048,512]{1,0:T(8,128)(2,1)}) fusion(s32[512]{0:T(512)S(1)} %add_select_fusion.9), kind=kLoop, calls=%fused_computation.78 | loop fusion | flops 19922944 | bytes 4196352 | tf_op jit(solution)/shard_map/convert
  407.5 65.5 %while.18 = (s32[]{:T(128)}, f32[512,2048]{1,0:T(8,128)}, f32[512,2048]{1,0:T(8,128)}, bf16[2,32,4096]{2,1,0:T(8,128)(2,1)S(1)}, s32[512]{0:T(512)S(1)}, /*index=5*/s32[512]{0:T(512)S(1)}, s32[]{:T(128)}, s32[]{:T(128)}) while((s32[]{:T(128)}, f32[512,2048]{1,0:T(8,128)}, f32[512,2048]{1,0:T(8,128)}, ...), condition=%wide.region_6.8_spmd.clone, body=%wide.region_5.7_spmd.clone.sunk | while | flops 18885636 | bytes 76052576 | solution.py:114
  412.0 6.1 %select_convert_fusion.4 = f32[512,4096]{1,0:T(8,128)} fusion(bf16[512,4096]{1,0:T(8,128)(2,1)} %gather_fusion, pred[512]{0:T(512)(128)(4,1)S(1)} %get-tuple-element.300), kind=kLoop, calls=%fused_computation.5.clone.1 | loop fusion | flops 4194304 | bytes 12583424 | tf_op jit(solution)/shard_map/while/body/eval_jaxpr/convert_element_type | solution.py:56
  428.5 9.8 %select_add_fusion.3 = (f32[512,2048]{1,0:T(8,128)}, f32[512,2048]{1,0:T(8,128)}) fusion(f32[512,2048]{1,0:T(8,128)} %get-tuple-element.330, f32[512,4096]{1,0:T(8,128)} %select_convert_fusion.4, f32[512,4096]{1,0:T(8,128)} %select_convert_fusion.5, pred[]{:T(512)S(6)} %compare.19, f32[512,2048]{1,0:T(8,128)} %get-tuple-element.329), kind=kLoop, calls=%fused_computation.7.clone.1 | loop fusion | flops 10485760 | bytes 33554432 | tf_op jit(solution)/shard_map/while/body/eval_jaxpr/add | solution.py:62
  442.7 6.1 %select_convert_fusion.4 = f32[512,4096]{1,0:T(8,128)} fusion(bf16[512,4096]{1,0:T(8,128)(2,1)} %gather_fusion, pred[512]{0:T(512)(128)(4,1)S(1)} %get-tuple-element.300), kind=kLoop, calls=%fused_computation.5.clone.1 | loop fusion | flops 4194304 | bytes 12583424 | tf_op jit(solution)/shard_map/while/body/eval_jaxpr/convert_element_type | solution.py:56
  459.2 13.7 %select_add_fusion.3 = (f32[512,2048]{1,0:T(8,128)}, f32[512,2048]{1,0:T(8,128)}) fusion(f32[512,2048]{1,0:T(8,128)} %get-tuple-element.330, f32[512,4096]{1,0:T(8,128)} %select_convert_fusion.4, f32[512,4096]{1,0:T(8,128)} %select_convert_fusion.5, pred[]{:T(512)S(6)} %compare.19, f32[512,2048]{1,0:T(8,128)} %get-tuple-element.329), kind=kLoop, calls=%fused_computation.7.clone.1 | loop fusion | flops 10485760 | bytes 33554432 | tf_op jit(solution)/shard_map/while/body/eval_jaxpr/add | solution.py:62
  (107 shorter events, 93.6 us)
Async XLA Ops:
  5.9 181.4 %copy-start.7 = (bf16[2,64,4096]{2,1,0:T(8,128)(2,1)}, bf16[2,64,4096]{2,1,0:T(8,128)(2,1)S(1)}, u32[]{:S(2)}) copy-start(bf16[2,64,4096]{2,1,0:T(8,128)(2,1)S(1)} %get-tuple-element.125) | copy-start | bytes 3145732
  22.3 16.7 %copy-start.5 = (s32[1,16,2]{1,2,0:T(2,128)S(1)}, s32[1,16,2]{1,2,0:T(2,128)}, u32[]{:S(2)}) copy-start(s32[1,16,2]{1,2,0:T(2,128)} %param.12) | copy-start | bytes 388
  204.7 18.9 %copy-start.8 = (bf16[2,64,4096]{2,1,0:T(8,128)(2,1)S(1)}, bf16[2,64,4096]{2,1,0:T(8,128)(2,1)}, u32[]{:S(2)}) copy-start(bf16[2,64,4096]{2,1,0:T(8,128)(2,1)} %copy-done.7) | copy-start | bytes 3145732
  273.2 70.2 %copy-start.3 = (f32[2,64,256]{2,1,0:T(8,128)S(1)}, f32[2,64,256]{2,1,0:T(8,128)}, u32[]{:S(2)}) copy-start(f32[2,64,256]{2,1,0:T(8,128)} %get-tuple-element.212) | copy-start | bytes 393220
  370.5 5.3 %copy-start.6 = (s32[1,16]{1,0:T(1,128)S(1)}, s32[1,16]{1,0:T(1,128)}, u32[]{:S(2)}) copy-start(s32[1,16]{1,0:T(1,128)} %param.13) | copy-start | bytes 196
  375.9 12.9 %copy-start.4 = (s32[2,512]{1,0:T(2,128)S(1)}, s32[2,512]{1,0:T(2,128)}, u32[]{:S(2)}) copy-start(s32[2,512]{1,0:T(2,128)} %param.14) | copy-start | bytes 12292
  383.8 23.4 %all-to-all-start = ((bf16[2,16,2,4096]{3,0,2,1:T(2,128)(2,1)}), bf16[2,16,2,4096]{3,0,2,1:T(2,128)(2,1)S(1)}, u32[]{:S(2)}, u32[]{:S(2)}) async-start(bf16[2,16,2,4096]{3,0,2,1:T(2,128)(2,1)} %broadcast_select_fusion.1), calls=%async_computation | async-start | bytes 1048576 | tf_op jit(solution)/shard_map/all_to_all | solution.py:106
  472.9 3.4 copy-start
  475.8 1.7 copy-start.1
  475.8 2.3 copy-start.2
  475.8 2.3 copy-start.9
where the time goes:
time: 491 us; the launch traced here: 482 us
  matrix products  270 us (55%)
  other arithmetic  79.6 us (16%)
  local copies, waits for them, and re-layouts  63.7 us (13%)
  blocking collectives  62.9 us (13%)
    dot_general x8, matrix products, body(): jnp.dot(flat_rows, sin_tab, preferred_element_type=jnp.float32)  134 us
    dot_general x8, matrix products, body(): jnp.dot(flat_rows, cos_tab, preferred_element_type=jnp.float32)  133 us
    psum x1, blocking collectives, body(): lax.psum((jnp.sum(real_part, axis=1), jnp.sum(imag_part, axis=1)), 'chan')  62.9 us
    another operation x4, other arithmetic  25.2 us
    concatenate x10, local copies, waits for them, and re-layouts, body(): imag_part = jnp.concatenate(imag_parts, axis=2)  23.6 us
    add x2, other arithmetic, accumulate(): imag_acc + (imag_a * real_b - real_a * imag_b)  23.5 us
    convert_element_type x2, other arithmetic, accumulate(): rows_b = jnp.take(arrived_rows, second_slot, axis=0).astype(jnp.float32)  12.2 us
    convert_element_type x2, other arithmetic, accumulate(): rows_a = jnp.take(arrived_rows, first_slot, axis=0).astype(jnp.float32)  12 us
  transfers between devices with their start and end apart: 1, of which 0 were waited for; matrix products, arithmetic and copies ran while one was open for 4% of the time, Pallas kernels for 0%

commit v1 on v0

v1 whole, which is shorter than its diff:
```python
import functools
import math

import jax
import jax.numpy as jnp
import numpy as np
from jax import lax
from jax.experimental import pallas as pl
from jax.experimental.pallas import tpu as pltpu
from jax.sharding import PartitionSpec as P

F = 2048
WLEN = 4096
BAND = 64
LAGS = 512
RAD = 16
T2 = WLEN // RAD
F2 = F // RAD
BLK = 2 * T2
VMEM_LIMIT = 56 * 2**20
MESH = pl.DeviceIdType.MESH


def tables():
    t2 = np.arange(T2)[:, None]
    f2 = np.arange(F2)[None, :]

    def trig(f1):
        angle = 2.0 * np.pi * ((t2 * (RAD * f2 + f1)) % WLEN) / WLEN
        return np.cos(angle), np.sin(angle)

    groups = []
    zero = np.zeros((T2, 2 * F2))
    cos0, sin0 = trig(0)
    cos8, sin8 = trig(RAD // 2)
    top = np.concatenate([cos0, -sin0, zero], 1)
    low = np.concatenate([zero, cos8, -sin8], 1)
    groups.append(np.concatenate([top, low], 0))
    for g in range(1, RAD // 2):
        cos_a, sin_a = trig(g)
        cos_b, sin_b = trig(RAD - g)
        top = np.concatenate([cos_a, -sin_a, cos_b, -sin_b], 1)
        low = np.concatenate([sin_a, cos_a, -sin_b, -cos_b], 1)
        groups.append(np.concatenate([top, low], 0))
    dft = np.stack(groups).astype(jnp.bfloat16)

    shifts = (np.arange(LAGS) - LAGS // 2) % WLEN
    lag = []
    for g in range(RAD // 2):
        for f1 in (g, RAD - g if g else RAD // 2):
            f = (RAD * np.arange(F2) + f1)[:, None]
            angle = 2.0 * np.pi * ((f * shifts[None, :]) % WLEN) / WLEN
            lag.append(np.cos(angle) / math.sqrt(F))
            lag.append(-np.sin(angle) / math.sqrt(F))
    lag = np.concatenate(lag, 0).astype(jnp.bfloat16)

    taper = 0.5 - 0.5 * np.cos(2.0 * np.pi * np.arange(WLEN) / WLEN)
    return dft, lag, taper.astype(np.float32).reshape(RAD, T2)


def cut_windows(rec_ref, starts_ref, win_ref):
    lane = lax.broadcasted_iota(jnp.int32, (rec_ref.shape[0], 128), 1)
    last = rec_ref.shape[1] - 128
    for w in range(win_ref.shape[0]):
        first = starts_ref[w]
        shift = first % 128
        base = first - shift

        def turned(m):
            at = pl.multiple_of(jnp.minimum(base + m * 128, last), 128)
            piece = rec_ref[:, pl.ds(at, 128)].astype(jnp.float32)
            return pltpu.roll(piece, (128 - shift) % 128, 1)

        here = turned(0)
        for m in range(WLEN // 128):
            after = turned(m + 1)
            win_ref[w, :, m * 128 : (m + 1) * 128] = jnp.where(lane < 128 - shift, here, after)
            here = after


def sum_channels(win_ref, part_ref):
    for w in range(win_ref.shape[0]):
        for j in range(RAD):
            total = jnp.sum(win_ref[w, :, j * T2 : (j + 1) * T2], axis=0, keepdims=True)
            part_ref[j, :, w * T2 : (w + 1) * T2] = total


def column(row):
    n = row.shape[1]
    down = lax.broadcasted_iota(jnp.int32, (n, n), 0)
    across = lax.broadcasted_iota(jnp.int32, (n, n), 1)
    return jnp.sum(jnp.where(down == across, row, 0.0), axis=1, keepdims=True)


def pick_rows(n, win_ref, rows_ref, count_ref, wide_ref, out_ref):
    chans = win_ref.shape[1]
    caps = rows_ref.shape[0]
    lane = lax.broadcasted_iota(jnp.int32, (n, chans), 1).astype(jnp.float32)
    for k in range(caps):
        picks = jnp.where(count_ref[...] > k, rows_ref[k : k + 1, :], -1).astype(jnp.float32)
        hot = jnp.where(lane == column(picks), 1.0, 0.0).astype(jnp.bfloat16)
        for w in range(2):
            for j in range(RAD):
                picked = jnp.dot(
                    hot,
                    win_ref[w, :, j * T2 : (j + 1) * T2].astype(jnp.bfloat16),
                    preferred_element_type=jnp.float32,
                )
                for half in range(2):
                    c = (k * 2 + w) * 2 + half
                    wide_ref[c, pl.ds(j, n, stride=RAD), :] = picked[:, half * 128 : (half + 1) * 128]
    for c in range(4 * caps):
        block = wide_ref[c].reshape(n, RAD, 128).astype(jnp.bfloat16)
        out_ref[c // 4, :, :, (c % 4) * 128 : (c % 4 + 1) * 128] = block


def cut_kernel(n, split, rec_ref, starts_ref, rows_ref, count_ref, out_ref, part_ref, win, wide, slab):
    cut_windows(rec_ref, starts_ref, win)
    if split == 1:
        sum_channels(win, part_ref)
    else:
        sum_channels(win, slab)
        width = slab.shape[2] // split
        for i in range(n):
            lo = (i % split) * width
            part_ref[i] = slab[i // split][:, lo : lo + width]
    pick_rows(n, win, rows_ref, count_ref, wide, out_ref)


def exchange_kernel(
    n, split, chans, outgoing, part, taper_ref, dft_hbm, white_ref,
    incoming, parts, total, slab, wide, lhs, spec, dft,
    row_send, row_recv, part_send, part_recv, sum_send, sum_recv, local_sem, dft_sem,
):
    me = lax.axis_index("chan")
    caps = outgoing.shape[0]
    dft_copy = pltpu.make_async_copy(dft_hbm, dft, dft_sem)
    dft_copy.start()

    def peer(d):
        return lax.rem(me + d, n)

    def remote(src, dst, send, recv, d):
        return pltpu.make_async_remote_copy(
            src_ref=src, dst_ref=dst, send_sem=send, recv_sem=recv,
            device_id={"chan": peer(d)}, device_id_type=MESH,
        )

    def row_copy(k, d):
        at = k * n + d
        return remote(outgoing.at[k, peer(d)], incoming.at[k, me], row_send.at[at], row_recv.at[at], d)

    def part_copy(d):
        return remote(part.at[peer(d)], parts.at[me], part_send.at[d], part_recv.at[d], d)

    def sum_copy(d):
        return remote(total.at[me], total.at[me], sum_send.at[d], sum_recv.at[d], d)

    def each(fn):
        def step(i, carry):
            fn(n // 2 + (2 * (i % 2) - 1) * ((i + 1) // 2))
            return carry

        lax.fori_loop(0, n - 1, step, 0)

    barrier = pltpu.get_barrier_semaphore()
    each(lambda d: pl.semaphore_signal(barrier, inc=1, device_id={"chan": peer(d)}, device_id_type=MESH))
    pl.semaphore_wait(barrier, n - 1)
    each(lambda d: part_copy(d).start())
    each(lambda d: row_copy(0, d).start())
    own = [pltpu.make_async_copy(outgoing.at[k, me], incoming.at[k, me], local_sem.at[k]) for k in range(caps)]
    for copy in own:
        copy.start()
    parts[me] = part[me]
    each(lambda d: part_copy(d).wait_recv())
    total[me] = jnp.sum(parts[...], axis=0)
    each(lambda d: sum_copy(d).start())
    for k in range(1, caps):
        each(functools.partial(lambda k, d: row_copy(k, d).start(), k))
    for copy in own:
        copy.wait()
    each(lambda d: sum_copy(d).wait_recv())
    width = slab.shape[2] // split
    for i in range(n):
        lo = (i % split) * width
        slab[i // split, :, lo : lo + width] = total[i] * (1.0 / chans)
    for k in range(caps):
        each(functools.partial(lambda k, d: row_copy(k, d).wait_recv(), k))
        short_dfts(n, k, incoming, slab, taper_ref, wide, lhs)
    dft_copy.wait()
    whiten(n, caps, lhs, dft, spec, white_ref)
    each(lambda d: part_copy(d).wait_send())
    each(lambda d: sum_copy(d).wait_send())
    for k in range(caps):
        each(functools.partial(lambda k, d: row_copy(k, d).wait_send(), k))


def real_dft(xs):
    size = len(xs)
    if size == 1:
        return [(xs[0], None)]
    even, odd = real_dft(xs[0::2]), real_dft(xs[1::2])
    if size == 2:
        return [(even[0][0] + odd[0][0], None), (even[0][0] - odd[0][0], None)]
    out = [None] * (size // 2 + 1)
    for k in range(size // 4 + 1):
        (er, ei), (or_, oi) = even[k], odd[k]
        c, s = math.cos(2 * math.pi * k / size), math.sin(2 * math.pi * k / size)
        if k == 0:
            tr, ti = or_, None
        elif 4 * k == size:
            tr, ti = oi, -or_
        elif oi is None:
            tr, ti = c * or_, -s * or_
        else:
            tr, ti = c * or_ + s * oi, c * oi - s * or_

        def plus(a, b):
            return b if a is None else a if b is None else a + b

        def minus(a, b):
            if b is None:
                return a
            return -b if a is None else a - b

        out[k] = (plus(er, tr), plus(ei, ti))
        if 4 * k == size:
            continue
        low = minus(ei, ti)
        out[size // 2 - k] = (minus(er, tr), None if low is None else -low)
    return out


def short_dfts(n, k, incoming, mean_ref, taper_ref, wide, lhs):
    for c in range(4):
        wide[k * 4 + c] = incoming[k, :, :, c * 128 : (c + 1) * 128].astype(jnp.float32).reshape(n * RAD, 128)
    for c in range(4):
        w, half = c // 2, c % 2
        cols = slice(half * 128, (half + 1) * 128)
        xs = []
        for j in range(RAD):
            mean = mean_ref[j, :, c * 128 : (c + 1) * 128]
            xs.append((wide[k * 4 + c, pl.ds(j, n, stride=RAD), :] - mean) * taper_ref[j : j + 1, cols])
        bins = real_dft(xs)
        rows = slice((k * 2 + w) * n, (k * 2 + w + 1) * n)
        right = slice(T2 + half * 128, T2 + (half + 1) * 128)
        lhs[0, rows, cols] = bins[0][0].astype(jnp.bfloat16)
        lhs[0, rows, right] = bins[RAD // 2][0].astype(jnp.bfloat16)
        for g in range(1, RAD // 2):
            lhs[g, rows, cols] = bins[g][0].astype(jnp.bfloat16)
            lhs[g, rows, right] = bins[g][1].astype(jnp.bfloat16)


def whiten(n, caps, lhs, dft_ref, spec, white):
    power = jnp.zeros((lhs.shape[1], F2), jnp.float32)
    for g in range(RAD // 2):
        block = jnp.dot(lhs[g], dft_ref[g], preferred_element_type=jnp.float32)
        spec[g] = block
        for q in range(4):
            piece = block[:, q * F2 : (q + 1) * F2]
            power = power + piece * piece
    lane = lax.broadcasted_iota(jnp.int32, power.shape, 1)
    for step in (1, 2):
        low = (lane // step) % 2 == 0
        power = power + jnp.where(low, pltpu.roll(power, F2 - step, 1), pltpu.roll(power, step, 1))
    scale = 1.0 / jnp.sqrt(power * (1.0 / (2 * BAND)) + 1e-06)
    for g in range(RAD // 2):
        for q in range(4):
            piece = (spec[g, :, q * F2 : (q + 1) * F2] * scale).astype(jnp.bfloat16)
            at = g * BLK + q * F2
            for kw in range(2 * caps):
                k, w = kw // 2, kw % 2
                white[w, k * n : (k + 1) * n, at : at + F2] = piece[kw * n : (kw + 1) * n]


def pairs_kernel(n, white, pairs_ref, live_ref, lag_hbm, out_ref, cross, lag, lag_sem):
    lag_copy = pltpu.make_async_copy(lag_hbm, lag, lag_sem)
    lag_copy.start()
    caps = white.shape[1] // n
    wide = max(128, caps * n)
    pair_cap = pairs_ref.shape[1]
    row = lax.broadcasted_iota(jnp.int32, (wide, pair_cap), 0)
    slot = jnp.where(row < caps * n, (row % n) * caps + row // n, caps * n)
    alive = lax.broadcasted_iota(jnp.int32, (1, pair_cap), 1) < live_ref[0]
    hots = []
    for member in range(2):
        index = jnp.where(alive, pairs_ref[member : member + 1, :], -1)
        hot = jnp.where(slot == index, 1.0, 0.0).T
        hots.append(hot[:, : caps * n].astype(jnp.bfloat16))
    chunk = 256
    for lo in range(0, pair_cap, chunk):
        hot_a, hot_b = hots[0][lo : lo + chunk], hots[1][lo : lo + chunk]
        for block in range(RAD):
            cols = slice(block * T2, (block + 1) * T2)
            real = imag = 0.0
            for w in range(2):
                a = jnp.dot(hot_a, white[w, :, cols], preferred_element_type=jnp.float32)
                b = jnp.dot(hot_b, white[w, :, cols], preferred_element_type=jnp.float32)
                ra, ia, rb, ib = a[:, :F2], a[:, F2:], b[:, :F2], b[:, F2:]
                real = real + (ra * rb + ia * ib)
                imag = imag + (ia * rb - ra * ib)
            cross[lo // chunk, :, block * T2 : block * T2 + F2] = (real * 0.5).astype(jnp.bfloat16)
            cross[lo // chunk, :, block * T2 + F2 : (block + 1) * T2] = (imag * 0.5).astype(jnp.bfloat16)
        if lo == 0:
            lag_copy.wait()
        out_ref[lo : lo + chunk, :] = jnp.dot(cross[lo // chunk], lag[...], preferred_element_type=jnp.float32)


def body(record, starts, send_rows, send_count, pair_slots, pair_count):
    local, windows = record.shape[0], starts.shape[0]
    n, caps = send_rows.shape[1], send_rows.shape[2]
    lanes = caps * windows * T2
    split = n // RAD
    width = windows * WLEN // n
    pair_cap = pair_slots.shape[1]
    f32, bf16 = jnp.float32, jnp.bfloat16
    vmem, smem = pl.BlockSpec(memory_space=pltpu.VMEM), pl.BlockSpec(memory_space=pltpu.SMEM)
    dma = pltpu.SemaphoreType.DMA
    hbm = pl.BlockSpec(memory_space=pl.ANY)
    rows_shape = (caps, n, RAD, windows * T2)
    part_shape = (n, 1, width)
    slab_shape = (RAD, 1, windows * T2)
    outgoing, part = pl.pallas_call(
        functools.partial(cut_kernel, n, split),
        out_shape=(jax.ShapeDtypeStruct(rows_shape, bf16), jax.ShapeDtypeStruct(part_shape, f32)),
        in_specs=[vmem, smem, vmem, vmem],
        out_specs=(vmem, vmem),
        scratch_shapes=[
            pltpu.VMEM((windows, local, WLEN), f32),
            pltpu.VMEM((lanes // 128, n * RAD, 128), f32),
            pltpu.VMEM(slab_shape, f32),
        ],
        compiler_params=pltpu.CompilerParams(vmem_limit_bytes=VMEM_LIMIT),
        name="cut",
    )(record, starts, send_rows[0].T, send_count)
    dft, lag, taper = tables()
    rows = caps * windows * n
    white = pl.pallas_call(
        functools.partial(exchange_kernel, n, split, local * n),
        out_shape=jax.ShapeDtypeStruct((windows, caps * n, 2 * F), bf16),
        in_specs=[vmem, vmem, vmem, hbm],
        out_specs=vmem,
        scratch_shapes=[
            pltpu.VMEM(rows_shape, bf16),
            pltpu.VMEM(part_shape, f32),
            pltpu.VMEM(part_shape, f32),
            pltpu.VMEM(slab_shape, f32),
            pltpu.VMEM((lanes // 128, n * RAD, 128), f32),
            pltpu.VMEM((RAD // 2, rows, BLK), bf16),
            pltpu.VMEM((RAD // 2, rows, BLK), f32),
            pltpu.VMEM(dft.shape, bf16),
            dma((caps * n,)), dma((caps * n,)), dma((n,)), dma((n,)), dma((n,)), dma((n,)), dma((caps,)), dma,
        ],
        compiler_params=pltpu.CompilerParams(
            collective_id=0, has_side_effects=True, vmem_limit_bytes=VMEM_LIMIT
        ),
        name="exchange",
    )(outgoing, part, jnp.asarray(taper), jnp.asarray(dft))
    return pl.pallas_call(
        functools.partial(pairs_kernel, n),
        out_shape=jax.ShapeDtypeStruct((pair_cap, LAGS), f32),
        in_specs=[vmem, vmem, smem, hbm],
        out_specs=vmem,
        scratch_shapes=[
            pltpu.VMEM((pair_cap // 256, 256, 2 * F), bf16),
            pltpu.VMEM(lag.shape, bf16),
            dma,
        ],
        compiler_params=pltpu.CompilerParams(vmem_limit_bytes=VMEM_LIMIT),
        name="pairs",
    )(white, pair_slots, pair_count, jnp.asarray(lag))


def solution(mesh):
    in_specs = (
        P(("groups", "chan"), None),
        P("groups"),
        P(("groups", "chan"), None, None),
        P(("groups", "chan"), None),
        P(None, ("groups", "chan")),
        P(("groups", "chan")),
    )
    out_specs = P(("groups", "chan"), None)
    return jax.shard_map(body, mesh=mesh, in_specs=in_specs, out_specs=out_specs, check_vma=False)
```

time: 491 us -> 38 us (0.08); the launches traced: 482 us -> 37.8 us
  matrix products: 270 us -> 0 us
  other arithmetic: 79.6 us -> 0 us
  local copies, waits for them, and re-layouts: 63.7 us -> 0 us
  blocking collectives: 62.9 us -> 0 us
  Pallas kernels: 0 us -> 37.1 us
    dot_general x17 -> x0, matrix products: 270 us -> none  [the longest x8 134 us: body(): jnp.dot(flat_rows, sin_tab, preferred_element_type=jnp.float32)]
    psum x1 -> x0, blocking collectives: 62.9 us -> none  [body(): lax.psum((jnp.sum(real_part, axis=1), jnp.sum(imag_part, axis=1)), 'chan')]
    pallas_call x0 -> x3, Pallas kernels: none -> 37.1 us  [the longest x1 24.9 us: body(): pl.pallas_call(functools.partial(exchange_kernel, n, split, local * n), o...]
    concatenate x21 -> x0, local copies, waits for them, and re-layouts: 34.2 us -> none  [the longest x10 23.6 us: body(): imag_part = jnp.concatenate(imag_parts, axis=2)]
    another operation x4 -> x0, other arithmetic: 25.2 us -> none
    convert_element_type x4 -> x0, other arithmetic: 24.2 us -> none  [the longest x2 12.2 us: accumulate(): rows_b = jnp.take(arrived_rows, second_slot, axis=0).astype(jnp.float32)]
    gather x11 -> x0, local copies, waits for them, and re-layouts: 24 us -> none  [the longest x2 8.79 us: accumulate(): rows_b = jnp.take(arrived_rows, second_slot, axis=0).astype(jnp.float32)]
    add x9 -> x0, other arithmetic: 23.5 us -> none  [the longest x2 23.5 us: accumulate(): imag_acc + (imag_a * real_b - real_a * imag_b)]
  transfers between devices with their start and end apart: 1 -> 0, of which waited for: 0 -> 0; matrix products, arithmetic and copies ran while one was open for 4% -> 0% of each run, Pallas kernels for 0% -> 0%
where the time goes in v1:
time: 38 us; the launch traced here: 37.8 us
  Pallas kernels  37.1 us (98%)
  between operations  0.66 us (2%)
    pallas_call x1, Pallas kernels, body(): pl.pallas_call(functools.partial(exchange_kernel, n, split, local * n), o...  24.9 us
    pallas_call x1, Pallas kernels, body(): pl.pallas_call(functools.partial(pairs_kernel, n), out_shape=jax.ShapeDty...  8.96 us
    pallas_call x1, Pallas kernels, body(): pl.pallas_call(functools.partial(cut_kernel, n, split), out_shape=(jax.Sh...  3.24 us

profile of v1, /device:TPU:0, one launch (start us, length us, event | category | flops | bytes accessed | tf_op | source)
XLA Modules:
  0.0 37.8 jit_solution(11633659524119589215)
XLA Ops:
  0.7 3.2 %cut.1 = (bf16[2,16,16,512]{3,2,1,0:T(8,128)(2,1)}, f32[16,1,512]{2,1,0:T(1,128)}) custom-call(bf16[64,12288]{1,0:T(8,128)(2,1)} %rec_ref.1, s32[2]{0:T(128)} %starts_ref.1, s32[2,16]{1,0:T(2,128)} %bitcast.3, s32[1,16]{1,0:T(1,128)} %count_ref.1), custom_call_target="tpu_custom_call" | custom-call | tf_op jit(solution)/shard_map/cut/pallas_call | solution.py:323
  3.9 24.9 %exchange.1.white = bf16[2,32,4096]{2,1,0:T(8,128)(2,1)} custom-call(bf16[2,16,16,512]{3,2,1,0:T(8,128)(2,1)} %get-tuple-element.7.outgoing, f32[16,1,512]{2,1,0:T(1,128)} %get-tuple-element.8.part, f32[16,256]{1,0:T(8,128)} %constant.6.clone.taper_ref, bf16[8,512,512]{2,1,0:T(8,128)(2,1)} %constant.7.clone.dft_hbm), custom_call_target="tpu_custom_call" | custom-call | tf_op jit(solution)/shard_map/exchange/pallas_call | solution.py:338
  28.8 9.0 %pairs.1 = f32[512,512]{1,0:T(8,128)} custom-call(bf16[2,32,4096]{2,1,0:T(8,128)(2,1)} %exchange.1.white, s32[2,512]{1,0:T(2,128)} %pairs_ref.1, s32[1]{0:T(128)S(6)} %copy.10.live_ref, bf16[4096,512]{1,0:T(8,128)(2,1)} %constant.8.clone.lag_hbm), custom_call_target="tpu_custom_call" | custom-call | tf_op jit(solution)/shard_map/pairs/pallas_call | solution.py:359

commit v2 on v1

--- a/solution.py
+++ b/solution.py
@@ -287,7 +287,7 @@
         index = jnp.where(alive, pairs_ref[member : member + 1, :], -1)
         hot = jnp.where(slot == index, 1.0, 0.0).T
         hots.append(hot[:, : caps * n].astype(jnp.bfloat16))
-    chunk = 256
+    chunk = pair_cap
     for lo in range(0, pair_cap, chunk):
         hot_a, hot_b = hots[0][lo : lo + chunk], hots[1][lo : lo + chunk]
         for block in range(RAD):
@@ -362,7 +362,7 @@
         in_specs=[vmem, vmem, smem, hbm],
         out_specs=vmem,
         scratch_shapes=[
-            pltpu.VMEM((pair_cap // 256, 256, 2 * F), bf16),
+            pltpu.VMEM((1, pair_cap, 2 * F), bf16),
             pltpu.VMEM(lag.shape, bf16),
             dma,
         ],

time: 38 us -> 38 us (level)
  no operation moved by 1% of the time
where the time goes in v2:
time: 38 us; the launch traced here: 37.8 us
  Pallas kernels  37.1 us (98%)
  between operations  0.66 us (2%)
    pallas_call x1, Pallas kernels, body(): pl.pallas_call(functools.partial(exchange_kernel, n, split, local * n), o...  24.9 us
    pallas_call x1, Pallas kernels, body(): pl.pallas_call(functools.partial(pairs_kernel, n), out_shape=jax.ShapeDty...  8.96 us
    pallas_call x1, Pallas kernels, body(): pl.pallas_call(functools.partial(cut_kernel, n, split), out_shape=(jax.Sh...  3.24 us

profile of v2, /device:TPU:0, one launch (start us, length us, event | category | flops | bytes accessed | tf_op | source)
XLA Modules:
  0.0 37.8 jit_solution(1153345781482670139)
XLA Ops:
  0.7 3.2 %cut.1 = (bf16[2,16,16,512]{3,2,1,0:T(8,128)(2,1)}, f32[16,1,512]{2,1,0:T(1,128)}) custom-call(bf16[64,12288]{1,0:T(8,128)(2,1)} %rec_ref.1, s32[2]{0:T(128)} %starts_ref.1, s32[2,16]{1,0:T(2,128)} %bitcast.3, s32[1,16]{1,0:T(1,128)} %count_ref.1), custom_call_target="tpu_custom_call" | custom-call | tf_op jit(solution)/shard_map/cut/pallas_call | solution.py:323
  3.9 24.9 %exchange.1.white = bf16[2,32,4096]{2,1,0:T(8,128)(2,1)} custom-call(bf16[2,16,16,512]{3,2,1,0:T(8,128)(2,1)} %get-tuple-element.7.outgoing, f32[16,1,512]{2,1,0:T(1,128)} %get-tuple-element.8.part, f32[16,256]{1,0:T(8,128)} %constant.6.clone.taper_ref, bf16[8,512,512]{2,1,0:T(8,128)(2,1)} %constant.7.clone.dft_hbm), custom_call_target="tpu_custom_call" | custom-call | tf_op jit(solution)/shard_map/exchange/pallas_call | solution.py:338
  28.8 9.0 %pairs.1 = f32[512,512]{1,0:T(8,128)} custom-call(bf16[2,32,4096]{2,1,0:T(8,128)(2,1)} %exchange.1.white, s32[2,512]{1,0:T(2,128)} %pairs_ref.1, s32[1]{0:T(128)S(6)} %copy.10.live_ref, bf16[4096,512]{1,0:T(8,128)(2,1)} %constant.8.clone.lag_hbm), custom_call_target="tpu_custom_call" | custom-call | tf_op jit(solution)/shard_map/pairs/pallas_call | solution.py:359
